TPU v7x, 128 devices: a whole 4x4x4 slice. The times are simulated.
128 devices in a mesh: shard: 16 (over y, z_hi, core), context: 8 (over x, z_lo).
Axes of the slice: x: 4, y: 4, z: 4 (z_hi: 2, z_lo: 2; z = z_hi * 2 + z_lo), core: 2. Of those that a mesh axis runs over, the one named last changes fastest.
Arguments:
- inputs: bfloat16 [16384, 1024], P(('shard', 'context')), may hold values from -6 to 6
- ln_gain: float32 [1024], replicated, may hold values from 0.1 to 1.9
- ln_bias: float32 [1024], replicated, may hold values from -2 to 2
- w_in: bfloat16 [7168, 1024], P('shard'), may hold values from -2 to 2
- b_in: float32 [7168], replicated, may hold values from -2 to 2
- w_out: bfloat16 [1024, 5120], P('shard'), may hold values from -2 to 2
- b_out: float32 [1024], replicated, may hold values from -2 to 2
- cotangent: bfloat16 [16384, 1024], P(('shard', 'context')), may hold values from -24 to 24
Outputs:
- out: bfloat16 [16384, 1024], P(('shard', 'context'))
- grad_inputs: bfloat16 [16384, 1024], P(('shard', 'context'))
- grad_ln_gain: float32 [1024], replicated
- grad_ln_bias: float32 [1024], replicated
- grad_w_in: float32 [7168, 1024], P('shard')
- grad_b_in: float32 [7168], replicated
- grad_w_out: float32 [1024, 5120], P('shard')
- grad_b_out: float32 [1024], replicated
All inputs are finite; a program needn't handle non-finite values.
Results may differ from a plain program's by a relative error of at most 0.018.
Values may be sent and summed in bfloat16 or wider, within the bound.
No kernel may reach another device: no remote copies, remote signals or barrier semaphores. Data moves between devices by JAX's collectives and lax.ppermute only.
A program may use at most 128 MiB of HBM per device.

v0:
```python
import jax
import jax.numpy as jnp
from jax import lax
from jax.sharding import PartitionSpec as P

D = 1024
H = 16
HD = 64
ROT = 32


epsilon = 1e-05


def layer_norm(rows_in, gain, shift):
    average = jnp.mean(rows_in, axis=-1, keepdims=True)
    centred = rows_in - average
    variance = jnp.mean(centred * centred, axis=-1, keepdims=True)
    return centred * lax.rsqrt(variance + epsilon) * gain + shift


def rotate(values, angles, turn):
    half = ROT // 2
    first = values[..., :half]
    second = values[..., half:ROT]
    remaining = values[..., ROT:]
    cosine = jnp.cos(angles)[:, None, :]
    sine = turn * jnp.sin(angles)[:, None, :]
    return jnp.concatenate(
        [first * cosine - second * sine, second * cosine + first * sine, remaining], axis=-1
    )


def against(left, right):
    return lax.dot_general(
        left, right, (((1,), (1,)), ((), ())), preferred_element_type=jnp.float32
    )


def over_tokens(left, right):
    return lax.dot_general(
        left, right, (((0,), (0,)), ((), ())), preferred_element_type=jnp.float32
    )


def gelu_tanh(values):
    return jax.nn.gelu(values, approximate=True)


def on_device(inputs, ln_gain, ln_bias, w_in, b_in, w_out, b_out, cotangent):
    row_count = inputs.shape[0]
    groups = lax.axis_size("context")
    seq_len = row_count * groups
    local_heads = H // groups
    block = min(512, seq_len)
    block_count = seq_len // block
    scale = HD ** (-0.5)
    rows_in = inputs.astype(jnp.float32)
    normed, norm_back = jax.vjp(layer_norm, rows_in, ln_gain, ln_bias)
    hidden = normed.astype(jnp.bfloat16)
    projected = against(hidden, lax.all_gather(w_in, "shard", axis=0, tiled=True))
    projected = projected + b_in
    positions = lax.axis_index("context") * row_count + jnp.arange(row_count)
    steps = jnp.arange(ROT // 2).astype(jnp.float32)
    angles = positions.astype(jnp.float32)[:, None] * (10000.0 ** (-2.0 * steps / ROT))[None, :]
    query = (
        rotate(projected[:, :D].reshape(row_count, H, HD), angles, 1.0)
        .reshape(row_count, D)
        .astype(jnp.bfloat16)
    )
    keys = (
        rotate(projected[:, D : 2 * D].reshape(row_count, H, HD), angles, 1.0)
        .reshape(row_count, D)
        .astype(jnp.bfloat16)
    )
    values = projected[:, 2 * D : 3 * D].astype(jnp.bfloat16)
    act = projected[:, 3 * D :]
    gated = gelu_tanh(act).astype(jnp.bfloat16)
    query_all, keys_all, values_all = (
        lax.all_to_all(query, "context", split_axis=1, concat_axis=0, tiled=True),
        lax.all_to_all(keys, "context", split_axis=1, concat_axis=0, tiled=True),
        lax.all_to_all(values, "context", split_axis=1, concat_axis=0, tiled=True),
    )
    query_heads = query_all.reshape(seq_len, local_heads, HD)
    keys_heads = keys_all.reshape(seq_len, local_heads, HD)
    values_heads = values_all.reshape(seq_len, local_heads, HD)
    key_place = jnp.arange(seq_len)

    def block_scores(index):
        first_row = index * block
        query_block = lax.dynamic_slice_in_dim(query_heads, first_row, block, 0)
        scores = (
            jnp.einsum("qhd,khd->hqk", query_block, keys_heads, preferred_element_type=jnp.float32)
            * scale
        )
        allowed = (first_row + jnp.arange(block))[:, None] >= key_place[None, :]
        return (query_block, jnp.where(allowed[None], scores, -1e30))

    def forward_block(index):
        query_block, scores = block_scores(index)
        largest = jnp.max(scores, axis=-1, keepdims=True)
        raised = jnp.exp(scores - largest)
        total_mass = jnp.sum(raised, axis=-1, keepdims=True)
        weights = (raised / total_mass).astype(jnp.bfloat16)
        result = jnp.einsum(
            "hqk,khd->qhd", weights, values_heads, preferred_element_type=jnp.float32
        )
        return (
            result.reshape(block, local_heads * HD).astype(jnp.bfloat16),
            (largest + jnp.log(total_mass))[..., 0],
        )

    attn_blocks, log_mass = lax.map(forward_block, jnp.arange(block_count))
    attn_heads = attn_blocks.reshape(seq_len, local_heads * HD)
    attn = lax.all_to_all(attn_heads, "context", split_axis=0, concat_axis=1, tiled=True)
    joined = jnp.concatenate([attn, gated], axis=1)
    mixed = against(joined, lax.all_gather(w_out, "shard", axis=0, tiled=True))
    out = (rows_in + mixed + b_out).astype(jnp.bfloat16)
    columns = cotangent
    grad_joined = jnp.dot(
        columns,
        lax.all_gather(w_out, "shard", axis=0, tiled=True),
        preferred_element_type=jnp.float32,
    )
    grad_attn = grad_joined[:, :D].astype(jnp.bfloat16)
    grad_act = jax.vjp(gelu_tanh, act)[1](grad_joined[:, D:])[0]
    grad_attn_all = lax.all_to_all(grad_attn, "context", split_axis=1, concat_axis=0, tiled=True)
    grad_attn_heads = grad_attn_all.reshape(seq_len, local_heads, HD)

    def backward_block(carry, item):
        grad_keys_sum, grad_values_sum = carry
        index, mass_block = item
        query_block, scores = block_scores(index)
        probs = jnp.exp(scores - mass_block[..., None])
        weights = probs.astype(jnp.bfloat16)
        grad_out_block = lax.dynamic_slice_in_dim(grad_attn_heads, index * block, block, 0)
        grad_values_sum = grad_values_sum + jnp.einsum(
            "hqk,qhd->khd", weights, grad_out_block, preferred_element_type=jnp.float32
        )
        grad_probs = jnp.einsum(
            "qhd,khd->hqk", grad_out_block, values_heads, preferred_element_type=jnp.float32
        )
        delta = jnp.sum(grad_probs * probs, axis=-1, keepdims=True)
        grad_scores = (probs * (grad_probs - delta)).astype(jnp.bfloat16)
        grad_query = (
            jnp.einsum("hqk,khd->qhd", grad_scores, keys_heads, preferred_element_type=jnp.float32)
            * scale
        )
        grad_keys_sum = (
            grad_keys_sum
            + jnp.einsum(
                "hqk,qhd->khd", grad_scores, query_block, preferred_element_type=jnp.float32
            )
            * scale
        )
        return (
            (grad_keys_sum, grad_values_sum),
            grad_query.reshape(block, local_heads * HD).astype(jnp.bfloat16),
        )

    zero_heads = jnp.zeros((seq_len, local_heads, HD), jnp.float32)
    (grad_keys_heads, grad_values_heads), grad_query_blocks = lax.scan(
        backward_block, (zero_heads, zero_heads), (jnp.arange(block_count), log_mass)
    )
    grad_query_all = grad_query_blocks.reshape(seq_len, local_heads * HD)
    grad_keys_all = grad_keys_heads.reshape(seq_len, local_heads * HD).astype(jnp.bfloat16)
    grad_values_all = grad_values_heads.reshape(seq_len, local_heads * HD).astype(jnp.bfloat16)
    grad_query, grad_keys, grad_values = (
        lax.all_to_all(grad_query_all, "context", split_axis=0, concat_axis=1, tiled=True),
        lax.all_to_all(grad_keys_all, "context", split_axis=0, concat_axis=1, tiled=True),
        lax.all_to_all(grad_values_all, "context", split_axis=0, concat_axis=1, tiled=True),
    )
    query_back = rotate(
        grad_query.astype(jnp.float32).reshape(row_count, H, HD), angles, -1.0
    ).reshape(row_count, D)
    keys_back = rotate(
        grad_keys.astype(jnp.float32).reshape(row_count, H, HD), angles, -1.0
    ).reshape(row_count, D)
    grad_proj = jnp.concatenate(
        [query_back, keys_back, grad_values.astype(jnp.float32), grad_act], axis=1
    ).astype(jnp.bfloat16)
    columns = grad_proj
    grad_normed = jnp.dot(
        columns,
        lax.all_gather(w_in, "shard", axis=0, tiled=True),
        preferred_element_type=jnp.float32,
    )
    columns = cotangent
    grad_w_out = lax.psum_scatter(
        over_tokens(columns, joined).astype(jnp.bfloat16), "shard", scatter_dimension=0, tiled=True
    ).astype(jnp.float32)
    columns = grad_proj
    grad_w_in = lax.psum_scatter(
        over_tokens(columns, hidden).astype(jnp.bfloat16), "shard", scatter_dimension=0, tiled=True
    ).astype(jnp.float32)
    grad_w_in, grad_w_out = (
        lax.psum(grad_w_in.astype(jnp.bfloat16), "context").astype(jnp.float32),
        lax.psum(grad_w_out.astype(jnp.bfloat16), "context").astype(jnp.float32),
    )
    grad_rows, grad_gain, grad_shift = norm_back(grad_normed)
    cot_rows = cotangent.astype(jnp.float32)
    grad_inputs = (cot_rows + grad_rows).astype(jnp.bfloat16)
    grad_b_in, grad_b_out, grad_gain, grad_shift = lax.psum(
        (
            jnp.sum(grad_proj.astype(jnp.float32), axis=0),
            jnp.sum(cot_rows, axis=0),
            grad_gain,
            grad_shift,
        ),
        ("shard", "context"),
    )
    return (out, grad_inputs, grad_gain, grad_shift, grad_w_in, grad_b_in, grad_w_out, grad_b_out)


def solution(mesh):
    in_specs = (
        P(("shard", "context"), None),
        P(),
        P(),
        P("shard", None),
        P(),
        P("shard", None),
        P(),
        P(("shard", "context"), None),
    )
    out_specs = (
        P(("shard", "context"), None),
        P(("shard", "context"), None),
        P(),
        P(),
        P("shard", None),
        P(),
        P("shard", None),
        P(),
    )
    return jax.shard_map(
        on_device, mesh=mesh, in_specs=in_specs, out_specs=out_specs, check_vma=False
    )
```

profile of v0, /device:TPU:0, one launch (start us, length us, event | category | flops | bytes accessed | tf_op | source)
XLA Modules:
  0.0 635.6 jit_solution(14361822912698500150)
XLA Ops:
  12.2 101.4 %all-gather.3.cloned.1.call-done = bf16[7168,1024]{1,0:T(8,128)(2,1)} async-done(((bf16[448,1024]{1,0:T(8,128)(2,1)}), bf16[7168,1024]{1,0:T(8,128)(2,1)}) %all-gather.3.cloned.1.call-update) | async-done | bytes 14680080 | tf_op jit(solution)/shard_map/all_gather | solution.py:61
  113.6 10.2 %convolution_add_fusion = f32[128,7168]{1,0:T(8,128)S(1)} fusion(bf16[7168,1024]{1,0:T(8,128)(2,1)} %all-gather.3.cloned.1.call-done, f32[7168]{0:T(1024)} %param.16, bf16[128,1024]{1,0:T(8,128)(2,1)} %param.12, f32[1024]{0:T(1024)} %param.14, f32[1024]{0:T(1024)} %param.13, f32[128]{0:T(128)S(1)} %fusion.61, f32[128]{0:T(128)S(1)} %broadcast_multiply_fusion.1), kind=kOutput, calls=%fused_computation.49 | convolution fusion | flops 1880752128 | bytes 18650112 | tf_op jit(solution)/shard_map/dot_general | solution.py:35
  127.1 4.3 all-to-all-start
  131.4 7.3 %all-to-all-done = bf16[128,8,128]{0,2,1:T(8,128)(2,1)S(1)} async-done(((bf16[128,8,128]{0,2,1:T(8,128)(2,1)}), bf16[128,8,128]{0,2,1:T(8,128)(2,1)S(1)}, u32[]{:S(2)}, u32[]{:S(2)}) %all-to-all-start) | async-done | bytes 262176 | tf_op jit(solution)/shard_map/all_to_all | solution.py:80
  138.8 3.4 all-to-all-start.1
  144.0 5.1 all-to-all-done.1
  149.1 4.1 all-to-all-start.2
  153.2 46.8 %all-gather.5.cloned.1.call-done = bf16[1024,5120]{1,0:T(8,128)(2,1)} async-done(((bf16[64,5120]{1,0:T(8,128)(2,1)}), bf16[1024,5120]{1,0:T(8,128)(2,1)}) %all-gather.5.cloned.1.call-update) | async-done | bytes 10485776 | tf_op jit(solution)/shard_map/all_gather | solution.py:117
  199.9 5.5 fusion.70
  210.0 16.7 %while.28 = (s32[]{:T(128)}, bf16[2,512,128]{2,1,0:T(8,128)(2,1)}, f32[2,2,512]{2,1,0:T(2,128)}, s32[2]{0:T(128)}, bf16[1024,2,64]{0,2,1:T(8,128)(2,1)}, /*index...) while((s32[]{:T(128)}, bf16[2,512,128]{2,1,0:T(8,128)(2,1)}, ...), condition=%wide.region_5.6_spmd.clone, body=%wide.region_2.5_spmd.clone.sunk | while | flops 281607680 | bytes 17076444 | solution.py:113
  226.7 4.2 all-to-all-start.3
  231.1 4.4 fusion.44
  235.5 3.0 all-to-all-done.3
  239.5 6.9 %convert_bitcast_fusion = bf16[1024,5120]{0,1:T(8,128)(2,1)} fusion(bf16[128,1024]{1,0:T(8,128)(2,1)S(1)} %copy-done.8, bf16[128,4096]{1,0:T(8,128)(2,1)} %get-tuple-element.272, bf16[128,1024]{1,0:T(8,128)(2,1)S(1)} %copy_bitcast_fusion.1), kind=kOutput, calls=%fused_computation.48 | convolution fusion | flops 1350041600 | bytes 12058624 | tf_op jit(solution)/shard_map/dot_general | solution.py:41
  246.4 13.7 %copy.87 = bf16[1024,5120]{1,0:T(8,128)(2,1)} copy(bf16[1024,5120]{0,1:T(8,128)(2,1)} %convert_bitcast_fusion) | data formatting | bytes 20971520
  260.9 3.4 all-to-all-start.4
  264.4 7.1 %all-to-all-done.4 = bf16[128,8,128]{2,0,1:T(8,128)(2,1)S(1)} async-done(((bf16[128,8,128]{2,0,1:T(8,128)(2,1)}), bf16[128,8,128]{2,0,1:T(8,128)(2,1)S(1)}, u32[]{:S(2)}, u32[]{:S(2)}) %all-to-all-start.4) | async-done | bytes 262176 | tf_op jit(solution)/shard_map/all_to_all | solution.py:127
  273.2 30.1 %while.29 = (s32[]{:T(128)}, f32[1024,2,64]{0,2,1:T(8,128)S(1)}, f32[1024,2,64]{0,2,1:T(8,128)}, bf16[2,512,128]{2,1,0:T(8,128)(2,1)}, s32[2]{0:T(128)S(1)}, /*i...) while((s32[]{:T(128)}, f32[1024,2,64]{0,2,1:T(8,128)S(1)}, ...), condition=%wide.region_8.9_spmd.clone, body=%wide.region_6.8_spmd.clone.sunk | while | flops 688127488 | bytes 55476516 | solution.py:162
  282.2 4.5 fusion.122
  297.3 4.5 fusion.122
  303.4 10.1 %all_to_all.110 = bf16[8,128,128]{1,2,0:T(8,128)(2,1)S(1)} all-to-all(bf16[8,128,128]{1,2,0:T(8,128)(2,1)S(1)} %copy.81), channel_id=1, replica_groups=mesh['shard'=16,'context'=8] {'context'}, dimensions={0} | all-to-all | bytes 524288 | tf_op jit(solution)/shard_map/all_to_all | solution.py:170
  313.5 3.4 all-to-all-start.5
  319.2 4.7 all-to-all-done.5
  323.8 3.4 all-to-all-start.7
  328.2 5.9 all-to-all-done.7
  334.2 7.6 %convolution_convert_fusion = bf16[7168,1024]{1,0:T(8,128)(2,1)} fusion(bf16[128,1024]{1,0:T(8,128)(2,1)S(1)} %copy-done.2, f32[1024]{0:T(1024)S(1)} %copy-done.12, f32[1024]{0:T(1024)S(1)} %copy-done.11, f32[128]{0:T(128)S(1)} %copy-done.18, f32[128]{0:T(128)S(1)} %copy-done.16, bf16[128,4096]{1,0:T(8,128)(2,1)S(1)} %copy-done.5, ...), kind=kOutput, calls=%fused_computation.47 | convolution fusion | flops 1894514688 | bytes 16786432 | tf_op jit(solution)/shard_map/dot_general | solution.py:41
  341.9 8.3 %fusion.68 = (f32[1024]{0:T(1024)S(1)}, f32[128]{0:T(128)S(1)}, f32[128,1024]{1,0:T(8,128)}) fusion(f32[1024]{0:T(1024)S(1)} %copy-done.11, f32[128]{0:T(128)S(1)} %copy-done.16, bf16[128,1024]{1,0:T(8,128)(2,1)S(1)} %copy-done.2, bf16[7168,1024]{1,0:T(8,128)(2,1)} %all-gather.3.cloned.1.call-done, bf16[128,4096]{1,0:T(8,128)(2,1)S(1)} %copy-done.5, ...), kind=kOutput, calls=%fused_computation.119 | convolution fusion | flops 1887173504 | bytes 17310720 | tf_op jit(solution)/shard_map/dot_general | solution.py:183
  350.2 25.7 %reduce-scatter.7.cloned.1.call-done = bf16[64,5120]{1,0:T(8,128)(2,1)} async-done(((bf16[1024,5120]{1,0:T(8,128)(2,1)}), bf16[64,5120]{1,0:T(8,128)(2,1)}) %reduce-scatter.7.cloned.1.call-update) | async-done | bytes 655376
  378.2 133.7 %reduce-scatter.5.cloned.1.call-done = bf16[448,1024]{1,0:T(8,128)(2,1)} async-done(((bf16[7168,1024]{1,0:T(8,128)(2,1)}), bf16[448,1024]{1,0:T(8,128)(2,1)}) %reduce-scatter.5.cloned.1.call-update) | async-done | bytes 917520 | tf_op jit(solution)/shard_map/reduce_scatter | solution.py:193
  515.7 70.5 %all-reduce = (f32[1024]{0:T(1024)}, f32[1024]{0:T(1024)}, f32[7168]{0:T(1024)}, f32[1024]{0:T(1024)}) all-reduce(f32[1024]{0:T(1024)S(1)} %get-tuple-element.223, f32[1024]{0:T(1024)S(1)} %get-tuple-element.225, f32[7168]{0:T(1024)S(1)} %convert_reduce_fusion, ...), channel_id=1, replica_groups=mesh['shard'=16,'context'=8] {'shard','context'}, use_global_device_ids=true, to_apply=%region_12.13 | all-reduce | flops 10240 | bytes 81920 | tf_op jit(solution)/shard_map/psum | solution.py:203
  586.2 8.4 %fusion.46 = bf16[128,1024]{1,0:T(8,128)(2,1)} fusion(bf16[1024,5120]{1,0:T(8,128)(2,1)} %all-gather.5.cloned.1.call-done, bf16[128,4096]{1,0:T(8,128)(2,1)S(1)} %copy-done.6, bf16[128,1024]{1,0:T(8,128)(2,1)} %copy-done.10, bf16[128,1024]{1,0:T(8,128)(2,1)S(1)} %copy-done.2, f32[1024]{0:T(1024)S(1)} %copy-done.21), kind=kOutput, calls=%fused_computation.65 | convolution fusion | flops 1345323008 | bytes 12324864 | tf_op jit(solution)/shard_map/dot_general | solution.py:35
  594.6 29.5 %all-reduce.4.cloned.1.call-done = (bf16[64,5120]{0,1:T(8,128)(2,1)}, bf16[448,1024]{1,0:T(8,128)(2,1)}) async-done(((bf16[64,5120]{0,1:T(8,128)(2,1)}, bf16[448,1024]{1,0:T(8,128)(2,1)}), (bf16[64,5120]{0,1:T(8,128)(2,1)}, bf16[448,1024]{1,0:T(8,128)(2,1)})) %all-reduce.4.cloned.1.call-update) | async-done | bytes 1572880 | tf_op jit(solution)/shard_map/psum | solution.py:198
  (158 shorter events, 67.4 us)
Async XLA Ops:
  7.2 106.4 %all-gather.3.cloned.1.call-start = ((), (), s32[]{:S(2)}) async-start(), calls=%async_computation.10 | async-start | bytes 15597568 | tf_op jit(solution)/shard_map/all_gather | solution.py:61
  7.9 192.0 %all-gather.5.cloned.1.call-start = ((), (), s32[]{:S(2)}) async-start(), calls=%async_computation.11 | async-start | bytes 11141120 | tf_op jit(solution)/shard_map/all_gather | solution.py:117
  9.8 114.0 %copy-start.15 = (f32[128]{0:T(128)}, f32[128]{0:T(128)S(1)}, u32[]{:S(2)}) copy-start(f32[128]{0:T(128)S(1)} %broadcast_multiply_fusion.1) | copy-start | bytes 1540
  11.5 112.3 %copy-start.17 = (f32[128]{0:T(128)}, f32[128]{0:T(128)S(1)}, u32[]{:S(2)}) copy-start(f32[128]{0:T(128)S(1)} %fusion.61) | copy-start | bytes 1540
  125.7 74.2 %copy-start.7 = (bf16[128,1024]{1,0:T(8,128)(2,1)S(1)}, bf16[128,1024]{1,0:T(8,128)(2,1)}, u32[]{:S(2)}) copy-start(bf16[128,1024]{1,0:T(8,128)(2,1)} %param.19) | copy-start | bytes 786436
  127.1 11.7 %all-to-all-start = ((bf16[128,8,128]{0,2,1:T(8,128)(2,1)}), bf16[128,8,128]{0,2,1:T(8,128)(2,1)S(1)}, u32[]{:S(2)}, u32[]{:S(2)}) async-start(bf16[128,8,128]{0,2,1:T(8,128)(2,1)} %bitcast.1), calls=%async_computation | async-start | bytes 524288 | tf_op jit(solution)/shard_map/all_to_all | solution.py:80
  138.8 10.3 %all-to-all-start.1 = ((bf16[128,8,128]{0,2,1:T(8,128)(2,1)}), bf16[128,8,128]{0,2,1:T(8,128)(2,1)S(1)}, u32[]{:S(2)}, u32[]{:S(2)}) async-start(bf16[128,8,128]{0,2,1:T(8,128)(2,1)} %bitcast.4), calls=%async_computation.1 | async-start | bytes 524288 | tf_op jit(solution)/shard_map/all_to_all | solution.py:81
  149.1 57.7 %all-to-all-start.2 = ((bf16[128,8,128]{2,0,1:T(8,128)(2,1)}), bf16[128,8,128]{2,0,1:T(8,128)(2,1)}, u32[]{:S(2)}, u32[]{:S(2)}) async-start(bf16[128,8,128]{2,0,1:T(8,128)(2,1)} %copy_bitcast_fusion.3), calls=%async_computation.2 | async-start | bytes 524288 | tf_op jit(solution)/shard_map/all_to_all | solution.py:82
  226.7 12.8 %copy-start.8 = (bf16[128,1024]{1,0:T(8,128)(2,1)S(1)}, bf16[128,1024]{1,0:T(8,128)(2,1)}, u32[]{:S(2)}) copy-start(bf16[128,1024]{1,0:T(8,128)(2,1)} %param.19) | copy-start | bytes 786436
  226.7 11.8 %all-to-all-start.3 = ((bf16[8,128,128]{2,1,0:T(8,128)(2,1)}), bf16[8,128,128]{2,1,0:T(8,128)(2,1)}, u32[]{:S(2)}, u32[]{:S(2)}) async-start(bf16[8,128,128]{2,1,0:T(8,128)(2,1)} %bitcast.140), calls=%async_computation.3 | async-start | bytes 524288 | tf_op jit(solution)/shard_map/all_to_all | solution.py:115
  230.9 145.0 %reduce-scatter.7.cloned.1.call-start = ((), (), s32[]{:S(2)}) async-start(), calls=%async_computation.13 | async-start | bytes 11141120
  239.5 6.9 %copy-start.10 = (bf16[128,1024]{1,0:T(8,128)(2,1)}, bf16[128,1024]{1,0:T(8,128)(2,1)S(1)}, u32[]{:S(2)}) copy-start(bf16[128,1024]{1,0:T(8,128)(2,1)S(1)} %copy_bitcast_fusion.1) | copy-start | bytes 786436
  260.1 13.0 %copy-start.13 = (f32[2,2,512]{2,1,0:T(2,128)S(1)}, f32[2,2,512]{2,1,0:T(2,128)}, u32[]{:S(2)}) copy-start(f32[2,2,512]{2,1,0:T(2,128)} %get-tuple-element.447) | copy-start | bytes 24580
  260.9 10.5 %all-to-all-start.4 = ((bf16[128,8,128]{2,0,1:T(8,128)(2,1)}), bf16[128,8,128]{2,0,1:T(8,128)(2,1)S(1)}, u32[]{:S(2)}, u32[]{:S(2)}) async-start(bf16[128,8,128]{2,0,1:T(8,128)(2,1)} %copy_bitcast_fusion.2), calls=%async_computation.4 | async-start | bytes 524288 | tf_op jit(solution)/shard_map/all_to_all | solution.py:127
  273.2 3.4 copy-start.4
  276.1 3.3 copy-start
  288.3 3.3 copy-start.4
  303.3 24.5 %copy-start.14 = (f32[128,16]{0,1:T(8,128)S(1)}, f32[128,16]{0,1:T(8,128)}, u32[]{:S(2)}) copy-start(f32[128,16]{0,1:T(8,128)} %get-tuple-element.289) | copy-start | bytes 24580
  313.5 10.3 %all-to-all-start.5 = ((bf16[8,128,128]{2,1,0:T(8,128)(2,1)}), bf16[8,128,128]{2,1,0:T(8,128)(2,1)S(1)}, u32[]{:S(2)}, u32[]{:S(2)}) async-start(bf16[8,128,128]{2,1,0:T(8,128)(2,1)} %bitcast.139), calls=%async_computation.5 | async-start | bytes 524288 | tf_op jit(solution)/shard_map/all_to_all | solution.py:169
  318.1 16.0 %copy-start.2 = (bf16[128,1024]{1,0:T(8,128)(2,1)S(1)}, bf16[128,1024]{1,0:T(8,128)(2,1)}, u32[]{:S(2)}) copy-start(bf16[128,1024]{1,0:T(8,128)(2,1)} %param.12) | copy-start | bytes 786436
  318.1 16.0 %copy-start.5 = (bf16[128,4096]{1,0:T(8,128)(2,1)S(1)}, bf16[128,4096]{1,0:T(8,128)(2,1)}, u32[]{:S(2)}) copy-start(bf16[128,4096]{1,0:T(8,128)(2,1)} %get-tuple-element.271) | copy-start | bytes 3145732
  318.2 16.0 %copy-start.11 = (f32[1024]{0:T(1024)S(1)}, f32[1024]{0:T(1024)}, u32[]{:S(2)}) copy-start(f32[1024]{0:T(1024)} %param.13) | copy-start | bytes 12292
  318.2 16.0 %copy-start.12 = (f32[1024]{0:T(1024)S(1)}, f32[1024]{0:T(1024)}, u32[]{:S(2)}) copy-start(f32[1024]{0:T(1024)} %param.14) | copy-start | bytes 12292
  318.2 16.0 %copy-start.16 = (f32[128]{0:T(128)S(1)}, f32[128]{0:T(128)}, u32[]{:S(2)}) copy-start(f32[128]{0:T(128)} %copy-done.15) | copy-start | bytes 1540
  318.2 16.0 %copy-start.18 = (f32[128]{0:T(128)S(1)}, f32[128]{0:T(128)}, u32[]{:S(2)}) copy-start(f32[128]{0:T(128)} %copy-done.17) | copy-start | bytes 1540
  323.8 10.3 %all-to-all-start.7 = ((bf16[8,128,128]{2,1,0:T(8,128)(2,1)}), bf16[8,128,128]{2,1,0:T(8,128)(2,1)S(1)}, u32[]{:S(2)}, u32[]{:S(2)}) async-start(bf16[8,128,128]{2,1,0:T(8,128)(2,1)} %copy.82), calls=%async_computation.7 | async-start | bytes 524288 | tf_op jit(solution)/shard_map/all_to_all | solution.py:171
  327.3 184.7 %reduce-scatter.5.cloned.1.call-start = ((), (), s32[]{:S(2)}) async-start(), calls=%async_computation.12 | async-start | bytes 15597568 | tf_op jit(solution)/shard_map/reduce_scatter | solution.py:193
  341.8 282.3 %all-reduce.4.cloned.1.call-start = ((), (), s32[]{:S(2)}) async-start(), calls=%async_computation.14 | async-start | bytes 4456448 | tf_op jit(solution)/shard_map/psum | solution.py:198
  350.2 161.7 %copy-start.20 = (f32[128]{0:T(128)S(1)}, f32[128]{0:T(128)}, u32[]{:S(2)}) copy-start(f32[128]{0:T(128)} %copy-done.19) | copy-start | bytes 1540
  350.2 163.4 %copy-start.9 = (bf16[128,1024]{1,0:T(8,128)(2,1)S(1)}, bf16[128,1024]{1,0:T(8,128)(2,1)}, u32[]{:S(2)}) copy-start(bf16[128,1024]{1,0:T(8,128)(2,1)} %param.19) | copy-start | bytes 786436
  350.2 236.0 %copy-start.6 = (bf16[128,4096]{1,0:T(8,128)(2,1)S(1)}, bf16[128,4096]{1,0:T(8,128)(2,1)}, u32[]{:S(2)}) copy-start(bf16[128,4096]{1,0:T(8,128)(2,1)} %get-tuple-element.272) | copy-start | bytes 3145732
  350.2 236.0 %copy-start.21 = (f32[1024]{0:T(1024)S(1)}, f32[1024]{0:T(1024)}, u32[]{:S(2)}) copy-start(f32[1024]{0:T(1024)} %param.18) | copy-start | bytes 12292
  (5 other events, 12.0 us)
Sparse Core Ops, SparseCore 0:
  10.4 103.1 all-gather.2
  116.0 83.9 all-gather.4
  260.3 115.5 reduce-scatter.6
  380.7 131.1 reduce-scatter.4
  514.9 109.1 all-reduce.3
where the time goes:
time: 638 us; the launch traced here: 636 us
  waiting for transfers between devices  371 us (58%)
  blocking collectives  80.6 us (13%)
  matrix products  76.4 us (12%)
  local copies, waits for them, and re-layouts  39.4 us (6%)
  starting transfers between devices  26.9 us (4%)
  other arithmetic  23.6 us (4%)
  between operations  14.3 us (2%)
    reduce_scatter x1, waiting for transfers between devices, on_device(): lax.psum_scatter(over_tokens(columns, hidden).astype(jnp.bfloat16), 'shar...  134 us
    all_gather x1, waiting for transfers between devices, on_device(): lax.all_gather(w_in, 'shard', axis=0, tiled=True)  101 us
    psum x1, blocking collectives, on_device(): lax.psum((jnp.sum(grad_proj.astype(jnp.float32), axis=0), jnp.sum(cot_row...  70.5 us
    all_gather x1, waiting for transfers between devices, on_device(): mixed = against(joined, lax.all_gather(w_out, 'shard', axis=0, tiled=True))  46.8 us
    psum x1, waiting for transfers between devices, on_device(): lax.psum(grad_w_out.astype(jnp.bfloat16), 'context').astype(jnp.float32)  29.5 us
    unnamed x6, waiting for transfers between devices  27.1 us
    unnamed x43, local copies, waits for them, and re-layouts  20.9 us
    dot_general x2, matrix products, against(): lax.dot_general(left, right, (((1,), (1,)), ((), ())), preferred_element_...  18.6 us
  transfers between devices with their start and end apart: 12, of which 11 were waited for; matrix products, arithmetic and copies ran while one was open for 14% of the time, Pallas kernels for 0%

commit v1 on v0

v1 whole, which is shorter than its diff:
```python
import functools

import jax
import jax.numpy as jnp
import numpy as np
from jax import lax
from jax.sharding import Mesh
from jax.sharding import PartitionSpec as P

D = 1024
FF = 4096
H = 16
HD = 64
ROT = 32
SEQ = 1024
EPS = 1e-05
BF = jnp.bfloat16
F32 = jnp.float32

SHARD = ("y", "zh", "core")
CONTEXT = ("x", "zl")

HEADS = ((0, 7), (8, 1), (14, 9), (6, 15), (12, 5), (4, 13), (10, 3), (2, 11))
UNITS_PER_SHARD = 7


def deal_units():
    columns = [[[], []] for _ in range(8)]
    qkv = [[kind * H + head for kind in range(3) for head in pair] for pair in HEADS]
    taken = [{unit // UNITS_PER_SHARD for unit in units} for units in qkv]
    order = []

    def place(unit):
        if unit == 112:
            return True
        shard, parity = unit // UNITS_PER_SHARD, unit % 2
        choices = sorted(range(8), key=lambda c: len(columns[c][0]) + len(columns[c][1]))
        for c in choices:
            if shard in taken[c] or len(columns[c][parity]) == 4:
                continue
            taken[c].add(shard)
            columns[c][parity].append(unit)
            if place(unit + 1):
                return True
            taken[c].remove(shard)
            columns[c][parity].pop()
        return False

    assert place(48)
    for c in range(8):
        pairs = [unit for pair in zip(*columns[c]) for unit in pair]
        order.append(qkv[c] + pairs)
    return np.array(order, np.int32)


UNITS = deal_units()
SLOT = UNITS // UNITS_PER_SHARD
SEND = np.zeros((16, 8), np.int32)
for _c in range(8):
    for _u in UNITS[_c]:
        SEND[_u // UNITS_PER_SHARD, _c] = _u % UNITS_PER_SHARD
HOME = np.zeros((112, 2), np.int32)
for _c in range(8):
    for _i, _u in enumerate(UNITS[_c]):
        HOME[_u] = (_c, _i)
COLUMN_UNITS = np.concatenate([np.array(HEADS, np.int32), UNITS[:, 6:] - 32], axis=1)
COLUMN_HOME = np.zeros((80, 2), np.int32)
for _c in range(8):
    for _i, _u in enumerate(COLUMN_UNITS[_c]):
        COLUMN_HOME[_u] = (_c, _i)


def swap(values, axis):
    return lax.ppermute(values, axis, [(0, 1), (1, 0)])


def ordered(index, mine, other, axis):
    first = jnp.where(index == 0, mine, other)
    second = jnp.where(index == 0, other, mine)
    return jnp.stack([first, second], axis=axis)


def spread(values, axes, count):
    copies = jnp.broadcast_to(values[None], (count,) + values.shape)
    return lax.all_to_all(copies, axes, 0, 0, tiled=True)


def gather_context(values):
    zl = lax.axis_index("zl")
    pair = ordered(zl, values, swap(values, "zl"), 0)
    return spread(pair, "x", 4).reshape((8,) + values.shape)


def scatter_context(parts):
    zl = lax.axis_index("zl")
    arrived = lax.all_to_all(parts.reshape((4, 2) + parts.shape[1:]), "x", 0, 0, tiled=True)
    total = jnp.sum(arrived.astype(F32), axis=0)
    mine = lax.dynamic_index_in_dim(total, zl, 0, keepdims=False)
    other = lax.dynamic_index_in_dim(total, 1 - zl, 0, keepdims=False)
    return mine + swap(other.astype(BF), "zl").astype(F32)


def gather_shard(values):
    core = lax.axis_index("core")
    near = spread(values, ("y", "zh"), 8)
    far = swap(near, "core")
    return ordered(core, near, far, 1).reshape((16,) + values.shape)


def scatter_shard(parts):
    core = lax.axis_index("core")
    halves = parts.reshape((8, 2) + parts.shape[1:])
    mine = lax.dynamic_index_in_dim(halves, core, 1, keepdims=False)
    other = lax.dynamic_index_in_dim(halves, 1 - core, 1, keepdims=False)
    near = (mine.astype(F32) + swap(other, "core").astype(F32)).astype(BF)
    arrived = lax.all_to_all(near, ("y", "zh"), 0, 0, tiled=True)
    return jnp.sum(arrived.astype(F32), axis=0)


def against(left, right):
    return lax.dot_general(left, right, (((1,), (1,)), ((), ())), preferred_element_type=F32)


def over_tokens(left, right):
    return lax.dot_general(left, right, (((0,), (0,)), ((), ())), preferred_element_type=F32)


def gelu_tanh(values):
    return jax.nn.gelu(values, approximate=True)


def normal(rows):
    average = jnp.mean(rows, axis=-1, keepdims=True)
    centred = rows - average
    variance = jnp.mean(centred * centred, axis=-1, keepdims=True)
    scale = lax.rsqrt(variance + EPS)
    return centred * scale, scale


def turn_tables():
    steps = jnp.arange(ROT // 2).astype(F32)
    angles = jnp.arange(SEQ).astype(F32)[:, None] * (10000.0 ** (-2.0 * steps / ROT))[None, :]
    cosine, sine = jnp.cos(angles), jnp.sin(angles)
    still = jnp.ones((SEQ, HD - ROT), F32)
    cosines = jnp.concatenate([cosine, cosine, still] * 2, axis=1)
    sines = jnp.concatenate([-sine, sine, 0.0 * still] * 2, axis=1)
    return cosines, sines


def turn(values, cosines, sines):
    lane = jnp.arange(2 * HD) % HD
    partner = jnp.where(lane < ROT // 2, jnp.roll(values, -(ROT // 2), 1), jnp.roll(values, ROT // 2, 1))
    return values * cosines + partner * sines


def on_device(inputs, ln_gain, ln_bias, w_in, b_in, w_out, b_out, cotangent):
    shard = lax.axis_index(SHARD)
    context = lax.axis_index(CONTEXT)
    scale = HD ** (-0.5)
    units = jnp.asarray(UNITS)[context]
    slots = jnp.asarray(SLOT)[context]

    x_all = gather_context(inputs).reshape(SEQ, D)
    unit = lax.dynamic_slice_in_dim(w_in, jnp.asarray(SEND)[shard, context] * 64, 64, 0)
    w_in_slots = gather_shard(unit)
    w_mine = w_in_slots[slots].reshape(896, D)
    column_units = jnp.asarray(COLUMN_UNITS)[context]
    w_out_part = w_out.reshape(64, 80, 64)[:, column_units].reshape(64, 640)
    w_out_mine = gather_shard(w_out_part).reshape(D, 640)
    cot_all = gather_context(cotangent).reshape(SEQ, D)
    bias = b_in.reshape(112, 64)[units].reshape(896)

    xhat, _ = normal(x_all.astype(F32))
    hidden = (xhat * ln_gain + ln_bias).astype(BF)
    projected = against(hidden, w_mine) + bias
    cosines, sines = turn_tables()
    query = turn(projected[:, :128], cosines, sines).astype(BF)
    keys = turn(projected[:, 128:256], cosines, sines).astype(BF)
    values = projected[:, 256:384].astype(BF)
    act = projected[:, 384:]
    gated = gelu_tanh(act).astype(BF)

    def heads(a):
        return a.reshape(SEQ, 2, HD)

    place = jnp.arange(SEQ)
    scores = jnp.einsum("qhd,khd->hqk", heads(query), heads(keys), preferred_element_type=F32) * scale
    scores = jnp.where((place[:, None] >= place[None, :])[None], scores, -1e30)
    raised = jnp.exp(scores - jnp.max(scores, axis=-1, keepdims=True))
    probs = raised / jnp.sum(raised, axis=-1, keepdims=True)
    weights = probs.astype(BF)
    attn = jnp.einsum("hqk,khd->qhd", weights, heads(values), preferred_element_type=F32).reshape(SEQ, 128).astype(BF)
    joined = jnp.concatenate([attn, gated], axis=1)
    out_part = against(joined, w_out_mine).astype(BF)
    mixed = scatter_context(out_part.reshape(8, 128, D))
    out = (inputs.astype(F32) + mixed + b_out).astype(BF)

    grad_joined = jnp.dot(cot_all, w_out_mine, preferred_element_type=F32)
    grad_attn = grad_joined[:, :128].astype(BF)
    grad_act = jax.vjp(gelu_tanh, act)[1](grad_joined[:, 128:])[0]
    grad_values = jnp.einsum("hqk,qhd->khd", weights, heads(grad_attn), preferred_element_type=F32).reshape(SEQ, 128)
    grad_probs = jnp.einsum("qhd,khd->hqk", heads(grad_attn), heads(values), preferred_element_type=F32)
    delta = jnp.sum(grad_probs * probs, axis=-1, keepdims=True)
    grad_scores = (probs * (grad_probs - delta)).astype(BF)
    grad_query = jnp.einsum("hqk,khd->qhd", grad_scores, heads(keys), preferred_element_type=F32) * scale
    grad_keys = jnp.einsum("hqk,qhd->khd", grad_scores, heads(query), preferred_element_type=F32) * scale
    grad_query = grad_query.reshape(SEQ, 128).astype(BF).astype(F32)
    grad_keys = grad_keys.reshape(SEQ, 128).astype(BF).astype(F32)
    grad_proj = jnp.concatenate(
        [turn(grad_query, cosines, -sines), turn(grad_keys, cosines, -sines), grad_values, grad_act], axis=1
    ).astype(BF)

    grad_normed = jnp.dot(grad_proj, w_mine, preferred_element_type=F32)
    grad_hidden = scatter_context(grad_normed.astype(BF).reshape(8, 128, D))
    grad_w_in = over_tokens(grad_proj, hidden).astype(BF).reshape(14, 64, D)
    grad_w_in = jnp.zeros((16, 64, D), BF).at[slots].set(grad_w_in)
    grad_w_out = over_tokens(cot_all, joined).astype(BF).reshape(16, 64, 640)
    grad_w_in = scatter_shard(grad_w_in).astype(BF)
    grad_w_out = scatter_shard(grad_w_out).astype(BF)
    grad_w_in = gather_context(grad_w_in)
    grad_w_out = gather_context(grad_w_out)
    homes = jnp.asarray(HOME[:, 0].reshape(16, 7))[shard]
    grad_w_in = grad_w_in[homes].reshape(448, D).astype(F32)
    grad_w_out = grad_w_out.reshape(8, 64, 10, 64).transpose(0, 2, 1, 3).reshape(80, 64, 64)
    grad_w_out = grad_w_out[COLUMN_HOME[:, 0] * 10 + COLUMN_HOME[:, 1]].transpose(1, 0, 2).reshape(64, 5120).astype(F32)

    small = jnp.concatenate(
        [
            jnp.sum(grad_proj.astype(F32), axis=0),
            jnp.sum(grad_normed * xhat, axis=0),
            jnp.sum(grad_normed, axis=0),
            jnp.sum(cotangent.astype(F32), axis=0),
        ]
    ).reshape(31, 128)
    small = jnp.sum(spread(small, SHARD, 16).reshape(16, 31, 128), axis=0)
    small = spread(small, CONTEXT, 8).reshape(8, 31 * 128)
    grad_b_in = small[:, :896].reshape(112, 64)[HOME[:, 0] * 14 + HOME[:, 1]].reshape(7168)
    rest = jnp.sum(small[:, 896:], axis=0)
    grad_gain, grad_shift, grad_b_out = rest[:D], rest[D : 2 * D], rest[2 * D :]

    own, own_scale = normal(inputs.astype(F32))
    pulled = grad_hidden * ln_gain
    grad_rows = (
        pulled
        - jnp.mean(pulled, axis=-1, keepdims=True)
        - own * jnp.mean(pulled * own, axis=-1, keepdims=True)
    ) * own_scale
    grad_inputs = (cotangent.astype(F32) + grad_rows).astype(BF)
    return (out, grad_inputs, grad_gain, grad_shift, grad_w_in, grad_b_in, grad_w_out, grad_b_out)


def solution(mesh):
    fine = Mesh(mesh.devices.reshape(4, 2, 2, 4, 2), SHARD + CONTEXT)
    rows = P(SHARD + CONTEXT, None)
    in_specs = (rows, P(), P(), P(SHARD, None), P(), P(SHARD, None), P(), rows)
    out_specs = (rows, rows, P(), P(), P(SHARD, None), P(), P(SHARD, None), P())
    return jax.shard_map(on_device, mesh=fine, in_specs=in_specs, out_specs=out_specs, check_vma=False)
```

time: 638 us -> 344 us (0.54)
  waiting for transfers between devices: 371 us -> 142 us
  blocking collectives: 80.6 us -> 0 us
  starting transfers between devices: 26.9 us -> 67.5 us
  matrix products: 76.4 us -> 47.8 us
  other arithmetic: 23.6 us -> 36.1 us
  between operations: 14.3 us -> 2.32 us
    all_gather x2 -> x0, waiting for transfers between devices: 148 us -> none  [the longest x1 101 us: on_device(): lax.all_gather(w_in, 'shard', axis=0, tiled=True)]
    reduce_scatter x1 -> x0, waiting for transfers between devices: 134 us -> none  [on_device(): lax.psum_scatter(over_tokens(columns, hidden).astype(jnp.bfloat16), 'shar...]
    all_to_all x7 -> x12, waiting for transfers between devices: 33.1 us -> 105 us  [the longest x8 72.9 us: spread(): return lax.all_to_all(copies, axes, 0, 0, tiled=True)]
    psum x1 -> x0, blocking collectives: 70.5 us -> none  [on_device(): lax.psum((jnp.sum(grad_proj.astype(jnp.float32), axis=0), jnp.sum(cot_row...]
    ppermute x0 -> x10, waiting for transfers between devices: none -> 37.8 us  [swap(): return lax.ppermute(values, axis, [(0, 1), (1, 0)])]
    all_to_all x7 -> x12, starting transfers between devices: 26.3 us -> 61.7 us  [the longest x8 38.7 us: spread(): return lax.all_to_all(copies, axes, 0, 0, tiled=True)]
    psum x1 -> x0, waiting for transfers between devices: 29.5 us -> none  [on_device(): lax.psum(grad_w_out.astype(jnp.bfloat16), 'context').astype(jnp.float32)]
    unnamed x6 -> x0, waiting for transfers between devices: 27.1 us -> none
  transfers between devices with their start and end apart: 12 -> 22, of which waited for: 11 -> 14; matrix products, arithmetic and copies ran while one was open for 14% -> 19% of each run, Pallas kernels for 0% -> 0%
where the time goes in v1:
time: 344 us; the launch traced here: 337 us
  waiting for transfers between devices  142 us (41%)
  starting transfers between devices  67.5 us (20%)
  matrix products  47.8 us (14%)
  local copies, waits for them, and re-layouts  41.3 us (12%)
  other arithmetic  36.1 us (10%)
    all_to_all x8, waiting for transfers between devices, spread(): return lax.all_to_all(copies, axes, 0, 0, tiled=True)  72.9 us
    all_to_all x8, starting transfers between devices, spread(): return lax.all_to_all(copies, axes, 0, 0, tiled=True)  38.7 us
    ppermute x10, waiting for transfers between devices, swap(): return lax.ppermute(values, axis, [(0, 1), (1, 0)])  37.8 us
    all_to_all x2, waiting for transfers between devices, scatter_context(): lax.all_to_all(parts.reshape((4, 2) + parts.shape[1:]), 'x', 0, 0, tiled=...  27.1 us
    all_to_all x2, starting transfers between devices, scatter_shard(): arrived = lax.all_to_all(near, ('y', 'zh'), 0, 0, tiled=True)  13.5 us
    all_to_all x2, starting transfers between devices, scatter_context(): lax.all_to_all(parts.reshape((4, 2) + parts.shape[1:]), 'x', 0, 0, tiled=...  9.45 us
    broadcast_in_dim x9, local copies, waits for them, and re-layouts, spread(): copies = jnp.broadcast_to(values[None], (count,) + values.shape)  8.83 us
    dot_general x2, matrix products, against(): lax.dot_general(left, right, (((1,), (1,)), ((), ())), preferred_element_...  8.68 us
  transfers between devices with their start and end apart: 22, of which 14 were waited for; matrix products, arithmetic and copies ran while one was open for 19% of the time, Pallas kernels for 0%

profile of v1, /device:TPU:0, one launch (start us, length us, event | category | flops | bytes accessed | tf_op | source)
XLA Modules:
  0.0 337.3 jit_solution(9318650690472525495)
XLA Ops:
  5.5 7.9 %all-to-all-start.2 = ((bf16[8,64,640]{2,1,0:T(8,128)(2,1)}), bf16[8,64,640]{2,1,0:T(8,128)(2,1)}, u32[]{:S(2)}, u32[]{:S(2)}) async-start(bf16[8,64,640]{2,1,0:T(8,128)(2,1)} %broadcast_in_dim.60), calls=%async_computation.2 | async-start | bytes 1310720 | tf_op jit(solution)/shard_map/all_to_all | solution.py:85
  15.5 10.2 %all-to-all-done.2 = bf16[8,64,640]{2,1,0:T(8,128)(2,1)} async-done(((bf16[8,64,640]{2,1,0:T(8,128)(2,1)}), bf16[8,64,640]{2,1,0:T(8,128)(2,1)}, u32[]{:S(2)}, u32[]{:S(2)}) %all-to-all-start.2) | async-done | bytes 655392 | tf_op jit(solution)/shard_map/all_to_all | solution.py:85
  26.7 3.6 %all-to-all-start.1 = ((bf16[8,64,1024]{2,1,0:T(8,128)(2,1)}), bf16[8,64,1024]{2,1,0:T(8,128)(2,1)S(1)}, u32[]{:S(2)}, u32[]{:S(2)}) async-start(bf16[8,64,1024]{2,1,0:T(8,128)(2,1)} %broadcast_in_dim.54), calls=%async_computation.1 | async-start | bytes 2097152 | tf_op jit(solution)/shard_map/all_to_all | solution.py:85
  33.2 16.6 %collective-permute-done = bf16[128,1024]{1,0:T(8,128)(2,1)S(1)} collective-permute-done((bf16[128,1024]{1,0:T(8,128)(2,1)S(1)}, bf16[128,1024]{1,0:T(8,128)(2,1)S(1)}, u32[]{:S(2)}, u32[]{:S(2)}) %collective-permute-start) | collective-permute-done | bytes 262176 | tf_op jit(solution)/shard_map/ppermute | solution.py:74
  49.7 4.3 %collective-permute-done.4 = bf16[128,1024]{1,0:T(8,128)(2,1)S(1)} collective-permute-done((bf16[128,1024]{1,0:T(8,128)(2,1)S(1)}, bf16[128,1024]{1,0:T(8,128)(2,1)S(1)}, u32[]{:S(2)}, u32[]{:S(2)}) %collective-permute-start.4) | collective-permute-done | bytes 262176 | tf_op jit(solution)/shard_map/ppermute | solution.py:74
  55.9 4.5 %all-to-all-start.4 = ((bf16[4,2,128,1024]{3,2,1,0:T(8,128)(2,1)}), bf16[4,2,128,1024]{3,2,1,0:T(8,128)(2,1)}, u32[]{:S(2)}, u32[]{:S(2)}) async-start(bf16[4,2,128,1024]{3,2,1,0:T(8,128)(2,1)} %broadcast_in_dim.61), calls=%async_computation.4 | async-start | bytes 4194304 | tf_op jit(solution)/shard_map/all_to_all | solution.py:85
  62.7 23.4 %all-to-all-done.4 = bf16[4,2,128,1024]{3,2,1,0:T(8,128)(2,1)} async-done(((bf16[4,2,128,1024]{3,2,1,0:T(8,128)(2,1)}), bf16[4,2,128,1024]{3,2,1,0:T(8,128)(2,1)}, u32[]{:S(2)}, u32[]{:S(2)}) %all-to-all-start.4) | async-done | bytes 2097184 | tf_op jit(solution)/shard_map/all_to_all | solution.py:85
  87.7 3.7 %all-to-all-start = ((bf16[4,2,128,1024]{3,2,1,0:T(8,128)(2,1)}), bf16[4,2,128,1024]{3,2,1,0:T(8,128)(2,1)S(1)}, u32[]{:S(2)}, u32[]{:S(2)}) async-start(bf16[4,2,128,1024]{3,2,1,0:T(8,128)(2,1)} %broadcast_in_dim.53), calls=%async_computation | async-start | bytes 4194304 | tf_op jit(solution)/shard_map/all_to_all | solution.py:85
  97.7 4.7 %fusion.89 = f32[1024,640]{0,1:T(8,128)} fusion(bf16[1024,1024]{1,0:T(8,128)(2,1)} %bitcast.31, bf16[1024,640]{1,0:T(8,128)(2,1)S(1)} %bitcast.176), kind=kOutput, calls=%fused_computation.191 | convolution fusion | flops 1342177280 | bytes 6029312 | tf_op jit(solution)/shard_map/dot_general | solution.py:198
  102.4 13.6 %all-to-all-done = bf16[4,2,128,1024]{3,2,1,0:T(8,128)(2,1)S(1)} async-done(((bf16[4,2,128,1024]{3,2,1,0:T(8,128)(2,1)}), bf16[4,2,128,1024]{3,2,1,0:T(8,128)(2,1)S(1)}, u32[]{:S(2)}, u32[]{:S(2)}) %all-to-all-start) | async-done | bytes 2097184 | tf_op jit(solution)/shard_map/all_to_all | solution.py:85
  124.0 3.5 %gather_fusion = bf16[14,64,1024]{2,1,0:T(8,128)(2,1)} fusion(bf16[16,64,1024]{2,1,0:T(8,128)(2,1)} %bitcast.165, s32[1024]{0:T(1024)S(1)} %pad_clamp_fusion.5), kind=kCustom, calls=%fused_computation | custom fusion | bytes 3670072 | tf_op jit(solution)/shard_map/gather | solution.py:166
  127.5 4.2 %broadcast_add_fusion = f32[1024,896]{0,1:T(8,128)S(1)} fusion(f32[896]{0:T(1024)S(1)} %add.220, bf16[1024,1024]{1,0:T(8,128)(2,1)} %bitcast.172, bf16[896,1024]{1,0:T(8,128)(2,1)} %bitcast.173), kind=kOutput, calls=%fused_computation.48 | convolution fusion | flops 1879965696 | bytes 7605760 | tf_op jit(solution)/shard_map/dot_general | solution.py:121
  137.7 7.9 %fusion.88 = (f32[2,1024]{1,0:T(2,128)S(1)}, f32[2,1024,1024]{1,2,0:T(8,128)}) fusion(pred[1024,1024]{0,1:T(8,128)(4,1)} %iota_compare_fusion, bf16[1024,2,64]{0,2,1:T(8,128)(2,1)} %bitcast.181, bf16[1024,2,64]{0,2,1:T(8,128)(2,1)S(1)} %bitcast.168), kind=kOutput, calls=%fused_computation.190 | convolution fusion | flops 276825088 | bytes 9969664 | tf_op jit(solution)/shard_map/sub | solution.py:189
  145.6 4.4 %fusion.19 = bf16[2,64,1024]{2,1,0:T(8,128)(2,1)S(1)} fusion(bf16[1024,2,64]{0,2,1:T(8,128)(2,1)S(1)} %bitcast.192, f32[2,1024,1024]{1,2,0:T(8,128)} %get-tuple-element.61, f32[2,1024]{1,0:T(2,128)S(1)} %get-tuple-element.60), kind=kOutput, calls=%fused_computation.57 | convolution fusion | flops 272760832 | bytes 8921088 | tf_op jit(solution)/shard_map/hqk,khd->qhd/dot_general | solution.py:192
  167.1 9.1 %all-to-all-start.10 = ((bf16[8,64,640]{2,1,0:T(8,128)(2,1)}), bf16[8,64,640]{2,1,0:T(8,128)(2,1)S(1)}, u32[]{:S(2)}, u32[]{:S(2)}) async-start(bf16[8,64,640]{2,1,0:T(8,128)(2,1)} %fusion.18), calls=%async_computation.10 | async-start | bytes 1310720 | tf_op jit(solution)/shard_map/all_to_all | solution.py:116
  176.2 7.8 %multiply_reduce_fusion.1 = (f32[1024]{0:T(1024)}, f32[1024]{0:T(1024)}, bf16[1024,1024]{1,0:T(8,128)(2,1)}, bf16[1024,1024]{1,0:T(8,128)(2,1)}) fusion(bf16[4,2,128,1024]{3,2,1,0:T(8,128)(2,1)S(1)} %all-to-all-done, f32[1024]{0:T(1024)S(1)} %bitcast.195, f32[1024]{0:T(1024)S(1)} %bitcast.194, f32[1024]{0:T(1024)} %param.19, f32[1024]{0:T(1024)S(1)} %copy-done.25, ...), kind=kOutput, calls=%fused_computation.16 | convolution fusion | flops 1896871936 | bytes 9986048 | tf_op jit(solution)/shard_map/dot_general | solution.py:213
  184.0 4.5 %all-to-all-done.10 = bf16[8,64,640]{2,1,0:T(8,128)(2,1)S(1)} async-done(((bf16[8,64,640]{2,1,0:T(8,128)(2,1)}), bf16[8,64,640]{2,1,0:T(8,128)(2,1)S(1)}, u32[]{:S(2)}, u32[]{:S(2)}) %all-to-all-start.10) | async-done | bytes 655392 | tf_op jit(solution)/shard_map/all_to_all | solution.py:116
  188.5 5.0 %all-to-all-start.5 = ((bf16[4,2,128,1024]{3,2,1,0:T(8,128)(2,1)}), bf16[4,2,128,1024]{3,2,1,0:T(8,128)(2,1)}, u32[]{:S(2)}, u32[]{:S(2)}) async-start(bf16[4,2,128,1024]{3,2,1,0:T(8,128)(2,1)} %bitcast.171), calls=%async_computation.5 | async-start | bytes 4194304 | tf_op jit(solution)/shard_map/all_to_all | solution.py:96
  193.5 4.9 %convolution_convert_fusion.1 = bf16[896,1024]{1,0:T(8,128)(2,1)} fusion(bf16[1024,1024]{1,0:T(8,128)(2,1)} %get-tuple-element.25, bf16[1024,512]{0,1:T(8,128)(2,1)S(1)} %copy-done.6, bf16[1024,128]{0,1:T(8,128)(2,1)S(1)} %bitcast.189, bf16[1024,128]{0,1:T(8,128)(2,1)S(1)} %copy-done.17, bf16[1024,128]{0,1:T(8,128)(2,1)S(1)} %get-tuple-element.30), kind=kOutput, calls=%fused_computation.49 | convolution fusion | flops 1887305728 | bytes 5767168 | tf_op jit(solution)/shard_map/dot_general | solution.py:125
  203.8 4.5 %convolution_convert_fusion = bf16[1024,1024]{1,0:T(8,128)(2,1)} fusion(bf16[1024,640]{1,0:T(8,128)(2,1)S(1)} %bitcast.177, bf16[1024,512]{0,1:T(8,128)(2,1)} %get-tuple-element.16, bf16[1024,128]{0,1:T(8,128)(2,1)S(1)} %bitcast.197), kind=kOutput, calls=%fused_computation.46 | convolution fusion | flops 1345847296 | bytes 4718592 | tf_op jit(solution)/shard_map/dot_general | solution.py:121
  208.2 11.5 %all-to-all-done.5 = bf16[4,2,128,1024]{3,2,1,0:T(8,128)(2,1)} async-done(((bf16[4,2,128,1024]{3,2,1,0:T(8,128)(2,1)}), bf16[4,2,128,1024]{3,2,1,0:T(8,128)(2,1)}, u32[]{:S(2)}, u32[]{:S(2)}) %all-to-all-start.5) | async-done | bytes 2097184 | tf_op jit(solution)/shard_map/all_to_all | solution.py:96
  219.7 4.5 %all-to-all-start.3 = ((bf16[4,2,128,1024]{3,2,1,0:T(8,128)(2,1)}), bf16[4,2,128,1024]{3,2,1,0:T(8,128)(2,1)}, u32[]{:S(2)}, u32[]{:S(2)}) async-start(bf16[4,2,128,1024]{3,2,1,0:T(8,128)(2,1)} %bitcast.170), calls=%async_computation.3 | async-start | bytes 4194304 | tf_op jit(solution)/shard_map/all_to_all | solution.py:96
  233.8 15.7 %all-to-all-done.3 = bf16[4,2,128,1024]{3,2,1,0:T(8,128)(2,1)} async-done(((bf16[4,2,128,1024]{3,2,1,0:T(8,128)(2,1)}), bf16[4,2,128,1024]{3,2,1,0:T(8,128)(2,1)}, u32[]{:S(2)}, u32[]{:S(2)}) %all-to-all-start.3) | async-done | bytes 2097184 | tf_op jit(solution)/shard_map/all_to_all | solution.py:96
  249.4 4.4 %all-to-all-start.8 = ((bf16[8,64,1024]{2,1,0:T(8,128)(2,1)}), bf16[8,64,1024]{2,1,0:T(8,128)(2,1)S(1)}, u32[]{:S(2)}, u32[]{:S(2)}) async-start(bf16[8,64,1024]{2,1,0:T(8,128)(2,1)} %fusion.13), calls=%async_computation.8 | async-start | bytes 2097152 | tf_op jit(solution)/shard_map/all_to_all | solution.py:116
  256.4 13.1 %collective-permute-done.3 = bf16[128,1024]{1,0:T(8,128)(2,1)S(1)} collective-permute-done((bf16[128,1024]{1,0:T(8,128)(2,1)S(1)}, bf16[128,1024]{1,0:T(8,128)(2,1)S(1)}, u32[]{:S(2)}, u32[]{:S(2)}) %collective-permute-start.3) | collective-permute-done | bytes 262176 | tf_op jit(solution)/shard_map/ppermute | solution.py:74
  271.3 7.6 %all-to-all-start.6 = ((f32[16,31,128]{2,1,0:T(8,128)}), f32[16,31,128]{2,1,0:T(8,128)S(1)}, u32[]{:S(2)}, u32[]{:S(2)}) async-start(f32[16,31,128]{2,1,0:T(8,128)} %broadcast_in_dim.63), calls=%async_computation.6 | async-start | bytes 524288 | tf_op jit(solution)/shard_map/all_to_all | solution.py:85
  280.0 8.2 %all-to-all-done.6 = f32[16,31,128]{2,1,0:T(8,128)S(1)} async-done(((f32[16,31,128]{2,1,0:T(8,128)}), f32[16,31,128]{2,1,0:T(8,128)S(1)}, u32[]{:S(2)}, u32[]{:S(2)}) %all-to-all-start.6) | async-done | bytes 253984 | tf_op jit(solution)/shard_map/all_to_all | solution.py:85
  294.6 3.8 %collective-permute-done.7 = bf16[64,1024]{1,0:T(8,128)(2,1)S(1)} collective-permute-done((bf16[64,1024]{1,0:T(8,128)(2,1)S(1)}, bf16[64,1024]{1,0:T(8,128)(2,1)S(1)}, u32[]{:S(2)}, u32[]{:S(2)}) %collective-permute-start.7) | collective-permute-done | bytes 131104 | tf_op jit(solution)/shard_map/ppermute | solution.py:74
  298.4 5.6 %all-to-all-done.11 = bf16[4,2,64,640]{3,2,1,0:T(8,128)(2,1)S(1)} async-done(((bf16[4,2,64,640]{3,2,1,0:T(8,128)(2,1)}), bf16[4,2,64,640]{3,2,1,0:T(8,128)(2,1)S(1)}, u32[]{:S(2)}, u32[]{:S(2)}) %all-to-all-start.11) | async-done | bytes 655392 | tf_op jit(solution)/shard_map/all_to_all | solution.py:85
  308.2 6.3 %all-to-all-done.7 = f32[8,31,128]{2,1,0:T(8,128)S(1)} async-done(((f32[8,31,128]{2,1,0:T(8,128)}), f32[8,31,128]{2,1,0:T(8,128)S(1)}, u32[]{:S(2)}, u32[]{:S(2)}) %all-to-all-start.7) | async-done | bytes 127008 | tf_op jit(solution)/shard_map/all_to_all | solution.py:85
  315.6 4.4 %all-to-all-start.9 = ((bf16[4,2,64,1024]{3,2,1,0:T(8,128)(2,1)}), bf16[4,2,64,1024]{3,2,1,0:T(8,128)(2,1)}, u32[]{:S(2)}, u32[]{:S(2)}) async-start(bf16[4,2,64,1024]{3,2,1,0:T(8,128)(2,1)} %broadcast_in_dim.66), calls=%async_computation.9 | async-start | bytes 2097152 | tf_op jit(solution)/shard_map/all_to_all | solution.py:85
  328.2 5.6 %all-to-all-done.9 = bf16[4,2,64,1024]{3,2,1,0:T(8,128)(2,1)} async-done(((bf16[4,2,64,1024]{3,2,1,0:T(8,128)(2,1)}), bf16[4,2,64,1024]{3,2,1,0:T(8,128)(2,1)}, u32[]{:S(2)}, u32[]{:S(2)}) %all-to-all-start.9) | async-done | bytes 1048608 | tf_op jit(solution)/shard_map/all_to_all | solution.py:85
  (203 shorter events, 96.2 us)
Async XLA Ops:
  0.6 14.8 %copy-start = (bf16[448,1024]{1,0:T(8,128)(2,1)S(1)}, bf16[448,1024]{1,0:T(8,128)(2,1)}, u32[]{:S(2)}) copy-start(bf16[448,1024]{1,0:T(8,128)(2,1)} %param.20) | copy-start | bytes 2752516
  5.5 20.1 %all-to-all-start.2 = ((bf16[8,64,640]{2,1,0:T(8,128)(2,1)}), bf16[8,64,640]{2,1,0:T(8,128)(2,1)}, u32[]{:S(2)}, u32[]{:S(2)}) async-start(bf16[8,64,640]{2,1,0:T(8,128)(2,1)} %broadcast_in_dim.60), calls=%async_computation.2 | async-start | bytes 1310720 | tf_op jit(solution)/shard_map/all_to_all | solution.py:85
  13.4 16.9 %copy-start.3 = (bf16[128,1024]{1,0:T(8,128)(2,1)S(1)}, bf16[128,1024]{1,0:T(8,128)(2,1)}, u32[]{:S(2)}) copy-start(bf16[128,1024]{1,0:T(8,128)(2,1)} %param.17) | copy-start | bytes 786436
  13.4 18.0 %copy-start.16 = (bf16[128,1024]{1,0:T(8,128)(2,1)S(1)}, bf16[128,1024]{1,0:T(8,128)(2,1)}, u32[]{:S(2)}) copy-start(bf16[128,1024]{1,0:T(8,128)(2,1)} %param.24) | copy-start | bytes 786436
  26.7 27.5 %all-to-all-start.1 = ((bf16[8,64,1024]{2,1,0:T(8,128)(2,1)}), bf16[8,64,1024]{2,1,0:T(8,128)(2,1)S(1)}, u32[]{:S(2)}, u32[]{:S(2)}) async-start(bf16[8,64,1024]{2,1,0:T(8,128)(2,1)} %broadcast_in_dim.54), calls=%async_computation.1 | async-start | bytes 2097152 | tf_op jit(solution)/shard_map/all_to_all | solution.py:85
  30.3 19.4 %collective-permute-start = (bf16[128,1024]{1,0:T(8,128)(2,1)S(1)}, bf16[128,1024]{1,0:T(8,128)(2,1)S(1)}, u32[]{:S(2)}, u32[]{:S(2)}) collective-permute-start(bf16[128,1024]{1,0:T(8,128)(2,1)S(1)} %copy-done.3), channel_id=1, source_target_pairs={{0,1},{1,0},{2,3},{3,2},{4,5},{5,4},{6,7},{7,6},{8,9},{9,8},{10,11... | collective-permute-start | bytes 786440 | tf_op jit(solution)/shard_map/ppermute | solution.py:74
  31.4 22.6 %collective-permute-start.4 = (bf16[128,1024]{1,0:T(8,128)(2,1)S(1)}, bf16[128,1024]{1,0:T(8,128)(2,1)S(1)}, u32[]{:S(2)}, u32[]{:S(2)}) collective-permute-start(bf16[128,1024]{1,0:T(8,128)(2,1)S(1)} %copy-done.16), channel_id=1, source_target_pairs={{0,1},{1,0},{2,3},{3,2},{4,5},{5,4},{6,7},{7,6},{8,9},{9,8},{10,11... | collective-permute-start | bytes 786440 | tf_op jit(solution)/shard_map/ppermute | solution.py:74
  55.9 30.1 %all-to-all-start.4 = ((bf16[4,2,128,1024]{3,2,1,0:T(8,128)(2,1)}), bf16[4,2,128,1024]{3,2,1,0:T(8,128)(2,1)}, u32[]{:S(2)}, u32[]{:S(2)}) async-start(bf16[4,2,128,1024]{3,2,1,0:T(8,128)(2,1)} %broadcast_in_dim.61), calls=%async_computation.4 | async-start | bytes 4194304 | tf_op jit(solution)/shard_map/all_to_all | solution.py:85
  62.6 32.5 %collective-permute-start.2 = (bf16[8,64,640]{2,1,0:T(8,128)(2,1)}, bf16[8,64,640]{2,1,0:T(8,128)(2,1)}, u32[]{:S(2)}, u32[]{:S(2)}) collective-permute-start(bf16[8,64,640]{2,1,0:T(8,128)(2,1)} %all-to-all-done.2), channel_id=1, source_target_pairs={{0,8},{8,0},{1,9},{9,1},{2,10},{10,2},{3,11},{11,3},{4,12},{12,4},... | collective-permute-start | bytes 1966088 | tf_op jit(solution)/shard_map/ppermute | solution.py:74
  87.7 28.4 %all-to-all-start = ((bf16[4,2,128,1024]{3,2,1,0:T(8,128)(2,1)}), bf16[4,2,128,1024]{3,2,1,0:T(8,128)(2,1)S(1)}, u32[]{:S(2)}, u32[]{:S(2)}) async-start(bf16[4,2,128,1024]{3,2,1,0:T(8,128)(2,1)} %broadcast_in_dim.53), calls=%async_computation | async-start | bytes 4194304 | tf_op jit(solution)/shard_map/all_to_all | solution.py:85
  94.9 26.2 %collective-permute-start.1 = (bf16[8,64,1024]{2,1,0:T(8,128)(2,1)}, bf16[8,64,1024]{2,1,0:T(8,128)(2,1)}, u32[]{:S(2)}, u32[]{:S(2)}) collective-permute-start(bf16[8,64,1024]{2,1,0:T(8,128)(2,1)} %copy-done.4), channel_id=1, source_target_pairs={{0,8},{8,0},{1,9},{9,1},{2,10},{10,2},{3,11},{11,3},{4,12},{12,4},... | collective-permute-start | bytes 3145736 | tf_op jit(solution)/shard_map/ppermute | solution.py:74
  102.4 16.5 %copy-start.25 = (f32[1024]{0:T(1024)S(1)}, f32[1024]{0:T(1024)}, u32[]{:S(2)}) copy-start(f32[1024]{0:T(1024)} %param.18) | copy-start | bytes 12292
  102.4 16.5 %copy-start.30 = (f32[1024]{0:T(1024)S(1)}, f32[1024]{0:T(1024)}, u32[]{:S(2)}) copy-start(f32[1024]{0:T(1024)} %param.19) | copy-start | bytes 12292
  163.8 2.3 collective-permute-start.8
  167.1 21.4 %all-to-all-start.10 = ((bf16[8,64,640]{2,1,0:T(8,128)(2,1)}), bf16[8,64,640]{2,1,0:T(8,128)(2,1)S(1)}, u32[]{:S(2)}, u32[]{:S(2)}) async-start(bf16[8,64,640]{2,1,0:T(8,128)(2,1)} %fusion.18), calls=%async_computation.10 | async-start | bytes 1310720 | tf_op jit(solution)/shard_map/all_to_all | solution.py:116
  188.5 31.2 %all-to-all-start.5 = ((bf16[4,2,128,1024]{3,2,1,0:T(8,128)(2,1)}), bf16[4,2,128,1024]{3,2,1,0:T(8,128)(2,1)}, u32[]{:S(2)}, u32[]{:S(2)}) async-start(bf16[4,2,128,1024]{3,2,1,0:T(8,128)(2,1)} %bitcast.171), calls=%async_computation.5 | async-start | bytes 4194304 | tf_op jit(solution)/shard_map/all_to_all | solution.py:96
  203.2 23.0 %collective-permute-start.6 = (bf16[8,64,1024]{2,1,0:T(8,128)(2,1)}, bf16[8,64,1024]{2,1,0:T(8,128)(2,1)}, u32[]{:S(2)}, u32[]{:S(2)}) collective-permute-start(bf16[8,64,1024]{2,1,0:T(8,128)(2,1)} %dynamic-slice_bitcast_fusion), channel_id=1, source_target_pairs={{0,8},{8,0},{1,9},{9,1},{2,10},{10,2},{3,11},{11,3},{4,12},{12,4},... | collective-permute-start | bytes 3145736 | tf_op jit(solution)/shard_map/ppermute | solution.py:74
  219.7 29.7 %all-to-all-start.3 = ((bf16[4,2,128,1024]{3,2,1,0:T(8,128)(2,1)}), bf16[4,2,128,1024]{3,2,1,0:T(8,128)(2,1)}, u32[]{:S(2)}, u32[]{:S(2)}) async-start(bf16[4,2,128,1024]{3,2,1,0:T(8,128)(2,1)} %bitcast.170), calls=%async_computation.3 | async-start | bytes 4194304 | tf_op jit(solution)/shard_map/all_to_all | solution.py:96
  229.5 49.5 %collective-permute-start.9 = (bf16[64,640]{1,0:T(8,128)(2,1)}, bf16[64,640]{1,0:T(8,128)(2,1)}, u32[]{:S(2)}, u32[]{:S(2)}) collective-permute-start(bf16[64,640]{1,0:T(8,128)(2,1)} %reduce_sum.185), channel_id=1, source_target_pairs={{0,1},{1,0},{2,3},{3,2},{4,5},{5,4},{6,7},{7,6},{8,9},{9,8},{10,11... | collective-permute-start | bytes 245768 | tf_op jit(solution)/shard_map/ppermute | solution.py:74
  231.7 24.5 %collective-permute-start.5 = (bf16[128,1024]{1,0:T(8,128)(2,1)S(1)}, bf16[128,1024]{1,0:T(8,128)(2,1)S(1)}, u32[]{:S(2)}, u32[]{:S(2)}) collective-permute-start(bf16[128,1024]{1,0:T(8,128)(2,1)S(1)} %fusion.56), channel_id=1, source_target_pairs={{0,1},{1,0},{2,3},{3,2},{4,5},{5,4},{6,7},{7,6},{8,9},{9,8},{10,11... | collective-permute-start | bytes 786440 | tf_op jit(solution)/shard_map/ppermute | solution.py:74
  249.4 21.2 %all-to-all-start.8 = ((bf16[8,64,1024]{2,1,0:T(8,128)(2,1)}), bf16[8,64,1024]{2,1,0:T(8,128)(2,1)S(1)}, u32[]{:S(2)}, u32[]{:S(2)}) async-start(bf16[8,64,1024]{2,1,0:T(8,128)(2,1)} %fusion.13), calls=%async_computation.8 | async-start | bytes 2097152 | tf_op jit(solution)/shard_map/all_to_all | solution.py:116
  253.8 15.7 %copy-start.27 = (f32[1024]{0:T(1024)S(1)}, f32[1024]{0:T(1024)}, u32[]{:S(2)}) copy-start(f32[1024]{0:T(1024)} %param.23) | copy-start | bytes 12292
  256.0 14.6 %copy-start.28 = (f32[1024]{0:T(1024)S(1)}, f32[1024]{0:T(1024)}, u32[]{:S(2)}) copy-start(f32[1024]{0:T(1024)} %get-tuple-element.8) | copy-start | bytes 12292
  256.0 14.6 %copy-start.29 = (f32[1024]{0:T(1024)S(1)}, f32[1024]{0:T(1024)}, u32[]{:S(2)}) copy-start(f32[1024]{0:T(1024)} %get-tuple-element.9) | copy-start | bytes 12292
  256.0 13.5 %collective-permute-start.3 = (bf16[128,1024]{1,0:T(8,128)(2,1)S(1)}, bf16[128,1024]{1,0:T(8,128)(2,1)S(1)}, u32[]{:S(2)}, u32[]{:S(2)}) collective-permute-start(bf16[128,1024]{1,0:T(8,128)(2,1)S(1)} %fusion.55), channel_id=1, source_target_pairs={{0,1},{1,0},{2,3},{3,2},{4,5},{5,4},{6,7},{7,6},{8,9},{9,8},{10,11... | collective-permute-start | bytes 786440 | tf_op jit(solution)/shard_map/ppermute | solution.py:74
  271.3 16.8 %all-to-all-start.6 = ((f32[16,31,128]{2,1,0:T(8,128)}), f32[16,31,128]{2,1,0:T(8,128)S(1)}, u32[]{:S(2)}, u32[]{:S(2)}) async-start(f32[16,31,128]{2,1,0:T(8,128)} %broadcast_in_dim.63), calls=%async_computation.6 | async-start | bytes 524288 | tf_op jit(solution)/shard_map/all_to_all | solution.py:85
  289.1 14.9 %all-to-all-start.11 = ((bf16[4,2,64,640]{3,2,1,0:T(8,128)(2,1)}), bf16[4,2,64,640]{3,2,1,0:T(8,128)(2,1)S(1)}, u32[]{:S(2)}, u32[]{:S(2)}) async-start(bf16[4,2,64,640]{3,2,1,0:T(8,128)(2,1)} %broadcast_in_dim.125), calls=%async_computation.11 | async-start | bytes 1310720 | tf_op jit(solution)/shard_map/all_to_all | solution.py:85
  292.8 5.6 %collective-permute-start.7 = (bf16[64,1024]{1,0:T(8,128)(2,1)S(1)}, bf16[64,1024]{1,0:T(8,128)(2,1)S(1)}, u32[]{:S(2)}, u32[]{:S(2)}) collective-permute-start(bf16[64,1024]{1,0:T(8,128)(2,1)S(1)} %reduce_sum.184), channel_id=1, source_target_pairs={{0,1},{1,0},{2,3},{3,2},{4,5},{5,4},{6,7},{7,6},{8,9},{9,8},{10,11... | collective-permute-start | bytes 393224 | tf_op jit(solution)/shard_map/ppermute | solution.py:74
  304.6 15.4 %copy-start.33 = (s32[112]{0:T(128)S(1)}, s32[112]{0:T(128)}, u32[]{:S(2)}) copy-start(s32[112]{0:T(128)} %constant.170) | copy-start | bytes 1348
  304.6 15.4 %copy-start.34 = (s32[80]{0:T(128)S(1)}, s32[80]{0:T(128)}, u32[]{:S(2)}) copy-start(s32[80]{0:T(128)} %constant.171) | copy-start | bytes 964
  304.6 9.9 %all-to-all-start.7 = ((f32[8,31,128]{2,1,0:T(8,128)}), f32[8,31,128]{2,1,0:T(8,128)S(1)}, u32[]{:S(2)}, u32[]{:S(2)}) async-start(f32[8,31,128]{2,1,0:T(8,128)} %broadcast_in_dim.64), calls=%async_computation.7 | async-start | bytes 262144 | tf_op jit(solution)/shard_map/all_to_all | solution.py:85
  315.6 18.1 %all-to-all-start.9 = ((bf16[4,2,64,1024]{3,2,1,0:T(8,128)(2,1)}), bf16[4,2,64,1024]{3,2,1,0:T(8,128)(2,1)}, u32[]{:S(2)}, u32[]{:S(2)}) async-start(bf16[4,2,64,1024]{3,2,1,0:T(8,128)(2,1)} %broadcast_in_dim.66), calls=%async_computation.9 | async-start | bytes 2097152 | tf_op jit(solution)/shard_map/all_to_all | solution.py:85
  (27 other events, 89.9 us)
